TPU v7x, 32 devices: a whole 2x2x4 slice. The times are simulated.
32 devices in a mesh: dom: 8 (over y, x, core), edge: 4 (over z).
Axes of the slice: x: 2, y: 2, z: 4, core: 2. Of those that a mesh axis runs over, the one named last changes fastest.
Arguments:
- edges: bfloat16 [32768, 512], P(('dom', 'edge')), may hold values from -6 to 6
- atoms: bfloat16 [1024, 256], P(('dom', 'edge')), may hold values from -6 to 6
- reverse: int32 [32768], P(('dom', 'edge')), may hold values from 0 to 32767, as said below
- atom_index: int32 [2, 32768], P(None, ('dom', 'edge')), may hold values from 0 to 127
- tile_source: int32 [512, 2], P(('dom', 'edge')), may hold values from 0 to 63
- tiles: bfloat16 [512, 64, 128], P(('dom', 'edge')), may hold values from -1 to 1
- weight_edge: bfloat16 [512, 512], replicated, may hold values from -0.25 to 0.25
- weight_down: bfloat16 [64, 512], replicated, may hold values from -0.25 to 0.25
- weight_up: bfloat16 [2, 64, 512], replicated, may hold values from -0.75 to 0.75
- weight_residual: bfloat16 [1, 2, 512, 512], replicated, may hold values from -0.25 to 0.25
- weight_message: bfloat16 [512, 256], replicated, may hold values from -0.25 to 0.25
- weight_atom: bfloat16 [2, 256, 256], replicated, may hold values from -0.375 to 0.375
- weight_join: bfloat16 [1024, 512], replicated, may hold values from -0.1875 to 0.1875
Outputs:
- new_edges: bfloat16 [32768, 512], P(('dom', 'edge'))
- new_atoms: bfloat16 [1024, 256], P(('dom', 'edge'))
Inputs may be any that keep to these rules, and one draw needn't show every extreme that they name: reverse is an involution without fixed points. The reverse of a row lies on a device of the same edge index. Besides its own partition, the rows of each partition have their reverses in exactly 4 other partitions; at most 128 rows of one device have their reverses in any one other partition, and some device reaches 128.
All inputs are finite; a program needn't handle non-finite values.
Results may differ from a plain program's by a relative error of at most 0.015.
Values may be sent and summed in bfloat16 or wider, within the bound.
No kernel may reach another device: no remote copies, remote signals or barrier semaphores. Data moves between devices by JAX's collectives and lax.ppermute only.
A program may use at most 64 MiB of HBM per device.

v0:
```python
import functools

import jax
import jax.numpy as jnp
from jax import lax
from jax.experimental import pallas as pl
from jax.experimental.pallas import tpu as pltpu
from jax.sharding import PartitionSpec as P

root_half = 0.7071067811865476
MIB = 1 << 20
CHUNK = 256


def product(operand, weights):
    return jnp.dot(operand, weights, preferred_element_type=jnp.float32)


def silu(value):
    halved = 0.5 * value
    return halved + halved * jnp.tanh(halved)


def as_column(row):
    wide = jnp.broadcast_to(row.astype(jnp.float32), (8, row.shape[1]))
    return jnp.transpose(wide)[:, :1].astype(jnp.int32)


def row_chunks(rows):
    step = min(CHUNK, rows)
    return [slice(at, at + step) for at in range(0, rows, step)]


def call(kernel, outs, args, *, smem=(), hbm=(), scratch=(), flops=0, nbytes=0, limit=24):
    def space(at):
        return pltpu.SMEM if at in smem else pltpu.HBM if at in hbm else pltpu.VMEM

    args = [
        pltpu.with_memory_space_constraint(arg, pltpu.HBM) if at in hbm else arg
        for at, arg in enumerate(args)
    ]
    return pl.pallas_call(
        kernel,
        out_shape=outs,
        in_specs=[pl.BlockSpec(memory_space=space(at)) for at in range(len(args))],
        out_specs=jax.tree.map(
            lambda out: pl.BlockSpec(
                memory_space=pltpu.HBM if out.memory_space == pltpu.HBM else pltpu.VMEM
            ),
            outs,
        ),
        scratch_shapes=list(scratch),
        compiler_params=pltpu.CompilerParams(vmem_limit_bytes=limit * MIB),
        cost_estimate=pl.CostEstimate(flops=flops, bytes_accessed=nbytes, transcendentals=0),
    )(*args)


def shaped(shape, dtype=jnp.bfloat16, space=pltpu.VMEM):
    return space(tuple(shape), dtype)


def narrow_kernel(
    edges_hbm, weight_hbm, down_hbm, atoms_hbm, out_ref, edges_ref, weight_ref, down_ref, sems
):
    half = edges_hbm.shape[0] // 2
    pieces = [
        slice(base + rows.start, base + rows.stop)
        for rows in row_chunks(half)
        for base in (0, half)
    ]
    copies = [
        pltpu.make_async_copy(weight_hbm, weight_ref, sems.at[0]),
        pltpu.make_async_copy(down_hbm, down_ref, sems.at[1]),
    ] + [
        pltpu.make_async_copy(edges_hbm.at[piece], edges_ref.at[piece], sems.at[2 + at])
        for at, piece in enumerate(pieces)
    ]
    for copy in [copies[0], copies[2], copies[3], copies[1]] + copies[4:]:
        copy.start()
    count, wide = atoms_hbm.shape
    lanes = out_ref.shape[1]
    atom_copies = [
        pltpu.make_async_copy(
            atoms_hbm.at[:, at * lanes : (at + 1) * lanes],
            out_ref.at[half + at * count : half + (at + 1) * count, :],
            sems.at[len(copies) + at],
        )
        for at in range(wide // lanes)
    ]
    for copy in atom_copies:
        copy.start()
    copies[0].wait()
    copies[1].wait()
    for at, rows in enumerate(row_chunks(half)):
        copies[2 + 2 * at].wait()
        copies[3 + 2 * at].wait()
        sides = []
        for side in range(2):
            hidden = silu(product(edges_ref[pieces[2 * at + side], :], weight_ref[...]))
            sides.append(
                silu(
                    lax.dot_general(
                        hidden.astype(jnp.bfloat16),
                        down_ref[...],
                        (((1,), (1,)), ((), ())),
                        preferred_element_type=jnp.float32,
                    )
                )
            )
        out_ref[rows, :] = jnp.concatenate(sides, axis=1).astype(jnp.bfloat16)
    for copy in atom_copies:
        copy.wait()


def index_kernel(domains, shards, operands, *refs):
    reverse_ref, narrow_ref = refs[:2]
    sources = refs[2 : 2 + operands]
    again_ref, send_ref, fetch_ref, local_ref = refs[2 + operands : 6 + operands]
    targets = refs[6 + operands : 6 + 2 * operands]
    sems = refs[-1]
    copies = [
        pltpu.make_async_copy(source, target, sems.at[at])
        for at, (source, target) in enumerate(zip(sources, targets))
    ]
    for copy in copies:
        copy.start()
    again_ref[...] = narrow_ref[...]
    rows = reverse_ref.shape[1]
    capacity = rows // domains
    half = capacity // 2
    slots = (domains - 1) * capacity
    own = lax.axis_index("dom")
    reverse = reverse_ref[...]
    holder = reverse // (rows * shards)
    source_row = lax.rem(reverse, rows)
    partner = holder ^ own
    source_column = as_column(source_row)
    member = (lax.broadcasted_iota(jnp.int32, (domains, rows), 0) == partner).astype(jnp.bfloat16)
    before = (
        lax.broadcasted_iota(jnp.int32, (rows, rows), 0)
        < lax.broadcasted_iota(jnp.int32, (rows, rows), 1)
    ).astype(jnp.bfloat16)
    place = jnp.sum(
        product(member, before) * member.astype(jnp.float32), axis=0, keepdims=True
    ).astype(jnp.int32)
    earlier = (source_column < source_row).astype(jnp.bfloat16)
    far_place = jnp.sum(
        product(member, earlier) * member.astype(jnp.float32), axis=0, keepdims=True
    ).astype(jnp.int32)

    def slot_of(at):
        part = (at >= half).astype(jnp.int32)
        slot = part * (slots // 2) + (domains - 1 - partner) * half + at - part * half
        return jnp.where(partner == 0, -1, slot)

    send_slot = slot_of(place)
    send_ref[...] = (
        lax.broadcasted_iota(jnp.int32, (slots, rows), 0) == send_slot
    ).astype(jnp.bfloat16)
    fetch_column = as_column(slot_of(far_place))
    fetch_ref[...] = (
        lax.broadcasted_iota(jnp.int32, (rows, slots), 1) == fetch_column
    ).astype(jnp.bfloat16)
    local_column = as_column(jnp.where(partner == 0, source_row, -1))
    local_ref[...] = (
        lax.broadcasted_iota(jnp.int32, (rows, rows), 1) == local_column
    ).astype(jnp.bfloat16)
    for copy in copies:
        copy.wait()


def mix_kernel(shards, count_parts, *refs):
    source_ref, tiles_ref = refs[:2]
    parts = refs[2 : 2 + count_parts]
    send_ref, trip_ref, atoms_ref = refs[2 + count_parts : 5 + count_parts]
    out_refs = refs[5 + count_parts : -1]
    held_ref = refs[-1]
    blocks, block_len, width = tiles_ref.shape
    count = width // block_len
    lines = held_ref.shape[0] // shards
    own_atoms = atoms_ref.shape[0] // shards
    atom_wide = atoms_ref.shape[1]
    lanes = held_ref.shape[1]
    me = lax.axis_index("edge")

    def keep(part, at):
        held_ref[at * lines : (at + 1) * lines, :] = part[:lines, :]
        for piece in range(atom_wide // lanes):
            start = lines + piece * own_atoms
            atoms_ref[
                at * own_atoms : (at + 1) * own_atoms, piece * lanes : (piece + 1) * lanes
            ] = part[start : start + own_atoms, :]

    if count_parts == shards:
        for part, at in zip(parts, distances(shards)):
            keep(part, at)
    else:
        for at in range(shards - 1):
            keep(parts[at], at)
        inner = (me > 0) & (me < shards - 1)
        pl.when(inner)(lambda: keep(parts[shards - 1], shards - 1))
        pl.when(jnp.logical_not(inner))(lambda: keep(parts[shards], shards - 1))
    half_blocks = blocks // 2
    channels = trip_ref.shape[1]
    for block in range(blocks):
        picks = []
        for tile in range(count):
            source = source_ref[block, tile]
            shard = source // blocks
            within = source - shard * blocks
            upper = within // half_blocks
            start = (shard ^ me) * lines + (within - upper * half_blocks) * block_len
            rows = held_ref[pl.ds(pl.multiple_of(start, block_len), block_len), :]
            picks.append(jnp.where(upper == 1, rows[:, channels:], rows[:, :channels]))
        mixed = product(tiles_ref[block], jnp.concatenate(picks, axis=0))
        trip_ref[block * block_len : (block + 1) * block_len, :] = mixed.astype(jnp.bfloat16)
    half_slots = send_ref.shape[0] // 2
    low = product(send_ref[:half_slots, :], trip_ref[...])
    high = product(send_ref[half_slots:, :], trip_ref[...])
    packed = jnp.concatenate([low, high], axis=1).astype(jnp.bfloat16)
    each = half_slots // len(out_refs)
    for at, out_ref in enumerate(out_refs):
        out_ref[...] = packed[at * each : (at + 1) * each, :]


def base_kernel(edges_ref, trip_ref, local_ref, up_ref, out_ref):
    channels = trip_ref.shape[1]
    for rows in row_chunks(edges_ref.shape[0]):
        picked = product(local_ref[rows, :], trip_ref[...]).astype(jnp.bfloat16)
        joined = product(trip_ref[rows, :], up_ref[0]) + product(picked, up_ref[1])
        out_ref[rows, :] = edges_ref[rows, :].astype(jnp.float32) + joined * root_half


def state_kernel(partners, *refs):
    base_ref, fetch_ref, up_ref, residual_ref, message_ref, index_ref = refs[:6]
    arrived = refs[6 : 6 + partners]
    state_ref, sums_ref, slots_ref = refs[6 + partners :]
    channels = up_ref.shape[1]
    each = arrived[0].shape[0]
    for at in range(partners):
        piece = arrived[at][...]
        slots_ref[at * each : (at + 1) * each, :] = piece[:, :channels]
        slots_ref[(partners + at) * each : (partners + at + 1) * each, :] = piece[:, channels:]
    part_atoms = sums_ref.shape[0]
    shards = lax.axis_size("edge")
    near = near_atoms(index_ref[1:2, :], part_atoms, shards)
    chosen = (
        lax.broadcasted_iota(jnp.int32, (part_atoms, near.shape[1]), 0) == near
    ).astype(jnp.bfloat16)
    chunks = row_chunks(base_ref.shape[0])
    gathered = None
    for first in range(0, len(chunks), 2):
        group = chunks[first : first + 2]
        picked = [product(fetch_ref[rows, :], slots_ref[...]).astype(jnp.bfloat16) for rows in group]
        states = [
            (base_ref[rows, :] + product(each, up_ref[1]) * root_half).astype(jnp.bfloat16)
            for rows, each in zip(group, picked)
        ]
        for layer in range(residual_ref.shape[0]):
            middles = [
                silu(product(each, residual_ref[layer, 0])).astype(jnp.bfloat16) for each in states
            ]
            branches = [silu(product(each, residual_ref[layer, 1])) for each in middles]
            states = [
                ((each.astype(jnp.float32) + branch) * root_half).astype(jnp.bfloat16)
                for each, branch in zip(states, branches)
            ]
        for rows, each in zip(group, states):
            state_ref[rows, :] = each
            term = product(chosen[:, rows], each)
            gathered = term if gathered is None else gathered + term
    sums_ref[...] = product(gathered.astype(jnp.bfloat16), message_ref[...]).astype(jnp.bfloat16)


def near_atoms(index, part_atoms, shards):
    count = part_atoms // shards
    holder = index // count
    return (holder ^ lax.axis_index("edge")) * count + lax.rem(index, count)


def side_kernel(shards, part_atoms, state_ref, join_ref, index_ref, out_ref, chosen_ref):
    width = join_ref.shape[0] - state_ref.shape[1]
    for rows in row_chunks(state_ref.shape[0]):
        out_ref[rows, :] = product(state_ref[rows, :], join_ref[width:, :])
    index = near_atoms(index_ref[...], part_atoms, shards)
    for end in range(2):
        column = as_column(index[end : end + 1, :])
        chosen_ref[:, end * part_atoms : (end + 1) * part_atoms] = (
            lax.broadcasted_iota(jnp.int32, (column.shape[0], part_atoms), 1) == column
        ).astype(jnp.bfloat16)


def final_kernel(shards, scale, *refs):
    sums = refs[:shards]
    atoms_ref, weight_ref, join_ref, state_ref, side_ref, chosen_ref = refs[shards : shards + 6]
    edges_hbm, own_hbm, table_ref, edges_ref, own_ref, sems = refs[shards + 6 :]
    part_atoms = atoms_ref.shape[0]
    count = part_atoms // shards
    total = sums[0][...].astype(jnp.float32)
    for by, part in list(zip(distances(shards), sums))[1:]:
        pieces = [part[(at ^ by) * count : ((at ^ by) + 1) * count, :] for at in range(shards)]
        total = total + jnp.concatenate(pieces, axis=0).astype(jnp.float32)
    scaled = (total * scale).astype(jnp.bfloat16)
    middle = silu(product(scaled, weight_ref[0])).astype(jnp.bfloat16)
    renewed = (atoms_ref[...].astype(jnp.float32) + product(middle, weight_ref[1])).astype(jnp.bfloat16)
    own_ref[...] = renewed[:count, :]
    own_copy = pltpu.make_async_copy(own_ref, own_hbm, sems.at[0])
    own_copy.start()
    width = renewed.shape[1]
    for end in range(2):
        table_ref[end * part_atoms : (end + 1) * part_atoms, :] = product(
            renewed, join_ref[end * width : (end + 1) * width, :]
        ).astype(jnp.bfloat16)
    copies = [own_copy]
    for at, rows in enumerate(row_chunks(state_ref.shape[0])):
        update = silu(product(chosen_ref[rows, :], table_ref[...]) + side_ref[rows, :])
        state = state_ref[rows, :].astype(jnp.float32)
        edges_ref[rows, :] = ((state + update) * root_half).astype(jnp.bfloat16)
        copies.append(
            pltpu.make_async_copy(edges_ref.at[rows], edges_hbm.at[rows], sems.at[1 + at])
        )
        copies[-1].start()
    for copy in copies:
        copy.wait()


def distances(shards):
    return [0, 1, 3, 2] if shards == 4 else list(range(shards))


def from_others(value, shards):
    return [value] + [
        lax.ppermute(value, "edge", [(at, at ^ by) for at in range(shards)])
        for by in distances(shards)[1:]
    ]


def by_relay(value, shards, between):
    if shards != 4:
        return from_others(value, shards), between(value)
    near = lax.ppermute(value, "edge", [(at, at ^ 1) for at in range(4)])
    far = lax.ppermute(value, "edge", [(at, at ^ 2) for at in range(4)])
    others = between(value)
    middle = lax.ppermute(others[0], "edge", [(1, 2), (2, 1)])
    relayed = lax.ppermute(far, "edge", [(2, 3), (1, 0)])
    return [value, near, far, middle, relayed], others


def body(
    edges,
    atoms,
    reverse,
    atom_index,
    tile_source,
    tiles,
    weight_edge,
    weight_down,
    weight_up,
    weight_residual,
    weight_message,
    weight_atom,
    weight_join,
):
    rows, wide = edges.shape
    channels = weight_down.shape[0]
    domains = lax.axis_size("dom")
    shards = lax.axis_size("edge")
    count, atom_wide = atoms.shape
    part_atoms = count * shards
    capacity = rows // domains
    partners = domains - 1
    slots = partners * capacity
    lines = rows // 2
    packed = 2 * channels

    narrow = call(
        narrow_kernel,
        shaped((lines + count * atom_wide // packed, packed)),
        (edges, weight_edge, weight_down, atoms),
        hbm=(0, 1, 2, 3),
        scratch=[
            pltpu.VMEM(edges.shape, jnp.bfloat16),
            pltpu.VMEM(weight_edge.shape, jnp.bfloat16),
            pltpu.VMEM(weight_down.shape, jnp.bfloat16),
            pltpu.SemaphoreType.DMA((2 + 2 * len(row_chunks(lines)) + atom_wide // packed,)),
        ],
        flops=2 * rows * wide * (wide + channels),
        nbytes=2 * (rows * wide + wide * wide),
    )
    later = (
        edges, tiles, weight_up, weight_residual, weight_message, weight_join, weight_atom, atom_index
    )
    def index_call(value):
        return call(
            functools.partial(index_kernel, domains, shards, len(later)),
            (
                shaped(value.shape),
                shaped((slots, rows)),
                shaped((rows, slots)),
                shaped((rows, rows)),
            )
            + tuple(shaped(each.shape, each.dtype) for each in later),
            (reverse.reshape(1, rows), value, *later),
            hbm=range(2, 2 + len(later)),
            scratch=[pltpu.SemaphoreType.DMA((len(later),))],
            flops=40 * rows * rows,
            nbytes=6 * rows * rows,
        )

    narrow_parts, (_, send, fetch, local, *later) = by_relay(narrow, shards, index_call)
    edges, tiles, weight_up, weight_residual, weight_message, weight_join, weight_atom, atom_index = later
    trip_out, all_atoms, *outgoing = call(
        functools.partial(mix_kernel, shards, len(narrow_parts)),
        (shaped((rows, channels)), shaped((part_atoms, atom_wide)))
        + (shaped((capacity // 2, packed)),) * partners,
        (tile_source, tiles, *narrow_parts, send),
        smem=(0,),
        scratch=[pltpu.VMEM((shards * lines, packed), jnp.bfloat16)],
        flops=2 * rows * rows * channels,
        nbytes=2 * rows * rows,
    )
    arrived = [
        lax.ppermute(block, "dom", [(at, at ^ (partners - place)) for at in range(domains)])
        for place, block in enumerate(outgoing)
    ]
    base = call(
        base_kernel,
        shaped((rows, wide), jnp.float32),
        (edges, trip_out, local, weight_up),
        flops=2 * rows * channels * (rows + 2 * wide),
        nbytes=2 * rows * rows + 6 * rows * wide,
    )
    state, sums = call(
        functools.partial(state_kernel, partners),
        (shaped((rows, wide)), shaped((part_atoms, atom_wide))),
        (base, fetch, weight_up, weight_residual, weight_message, atom_index, *arrived),
        scratch=[pltpu.VMEM((slots, channels), jnp.bfloat16)],
        flops=4 * rows * wide * wide,
        nbytes=8 * rows * wide,
    )
    sums_parts = from_others(sums, shards)
    side, chosen = call(
        functools.partial(side_kernel, shards, part_atoms),
        (shaped((rows, wide), jnp.float32), shaped((rows, 2 * part_atoms))),
        (state, weight_join, atom_index),
        flops=2 * rows * wide * wide,
        nbytes=8 * rows * wide,
    )
    return call(
        functools.partial(final_kernel, shards, (rows // count) ** -0.5),
        (shaped((rows, wide), space=pltpu.HBM), shaped((count, atom_wide), space=pltpu.HBM)),
        (*sums_parts, all_atoms, weight_atom, weight_join, state, side, chosen),
        scratch=[
            pltpu.VMEM((2 * part_atoms, wide), jnp.bfloat16),
            pltpu.VMEM((rows, wide), jnp.bfloat16),
            pltpu.VMEM((count, atom_wide), jnp.bfloat16),
            pltpu.SemaphoreType.DMA((1 + len(row_chunks(rows)),)),
        ],
        flops=4 * rows * part_atoms * wide,
        nbytes=8 * rows * wide,
    )


def solution(mesh):
    split = P(("dom", "edge"))
    placed = (
        P(("dom", "edge"), None),
        P(("dom", "edge"), None),
        split,
        P(None, ("dom", "edge")),
        P(("dom", "edge"), None),
        P(("dom", "edge"), None, None),
    ) + (P(),) * 7
    return jax.shard_map(
        body,
        mesh=mesh,
        in_specs=placed,
        out_specs=(P(("dom", "edge"), None), P(("dom", "edge"), None)),
        check_vma=False,
    )
```

profile of v0, /device:TPU:0, one launch (start us, length us, event | category | flops | bytes accessed | tf_op | source)
XLA Modules:
  0.0 55.3 jit_solution(18291876709548618401)
XLA Ops:
  0.6 3.0 %shard_map.140.refs_1_.refs_2_ = bf16[576,128]{1,0:T(8,128)(2,1)S(1)} custom-call(bf16[1024,512]{1,0:T(8,128)(2,1)} %refs_2_.1, bf16[512,512]{1,0:T(8,128)(2,1)} %weight_hbm.1, bf16[64,512]{1,0:T(8,128)(2,1)} %down_hbm.1, bf16[32,256]{1,0:T(8,128)(2,1)} %atoms_hbm.1), custom_call_target="tpu_custom_call" | custom-call | flops 603979776 | bytes 1572864 | tf_op jit(solution)/shard_map/pallas_call | solution.py:42
  3.7 4.1 %collective-permute-start.1 = (bf16[576,128]{1,0:T(8,128)(2,1)S(1)}, bf16[576,128]{1,0:T(8,128)(2,1)}, u32[]{:S(2)}, u32[]{:S(2)}) collective-permute-start(bf16[576,128]{1,0:T(8,128)(2,1)S(1)} %shard_map.140.refs_1_.refs_2_), channel_id=1, source_target_pairs={{0,2},{1,3},{2,0},{3,1},{4,6},{5,7},{6,4},{7,5},{8,10},{9,11},{10,... | collective-permute-start | bytes 442376 | tf_op jit(solution)/shard_map/ppermute | solution.py:342
  7.8 1.6 %collective-permute-start = (bf16[576,128]{1,0:T(8,128)(2,1)S(1)}, bf16[576,128]{1,0:T(8,128)(2,1)}, u32[]{:S(2)}, u32[]{:S(2)}) collective-permute-start(bf16[576,128]{1,0:T(8,128)(2,1)S(1)} %shard_map.140.refs_1_.refs_2_), channel_id=1, source_target_pairs={{0,1},{1,0},{2,3},{3,2},{4,5},{5,4},{6,7},{7,6},{8,9},{9,8},{10,11... | collective-permute-start | bytes 442376 | tf_op jit(solution)/shard_map/ppermute | solution.py:341
  9.3 3.3 %shard_map.141 = (bf16[576,128]{1,0:T(8,128)(2,1)}, bf16[896,1024]{1,0:T(8,128)(2,1)S(1)}, bf16[1024,896]{1,0:T(8,128)(2,1)S(1)}, bf16[1024,1024]{1,0:T(8,128)(2...) custom-call(s32[1,1024]{1,0:T(1,128)S(1)} %bitcast.1, ...), custom_call_target="tpu_custom_call" | custom-call | flops 41943040 | bytes 6291456 | tf_op jit(solution)/shard_map/pallas_call | solution.py:42
  12.7 1.2 %copy-done = bf16[896,1024]{1,0:T(8,128)(2,1)} copy-done((bf16[896,1024]{1,0:T(8,128)(2,1)}, bf16[896,1024]{1,0:T(8,128)(2,1)S(1)}, u32[]{:S(2)}) %copy-start) | copy-done | bytes 1835032
  13.9 1.3 %copy-done.2 = bf16[1024,896]{1,0:T(8,128)(2,1)} copy-done((bf16[1024,896]{1,0:T(8,128)(2,1)}, bf16[1024,896]{1,0:T(8,128)(2,1)S(1)}, u32[]{:S(2)}) %copy-start.2) | copy-done | bytes 1835032
  15.2 1.0 %copy-done.4 = bf16[1,2,512,512]{3,2,1,0:T(8,128)(2,1)} copy-done((bf16[1,2,512,512]{3,2,1,0:T(8,128)(2,1)}, bf16[1,2,512,512]{3,2,1,0:T(8,128)(2,1)S(1)}, u32[]{:S(2)}) %copy-start.4) | copy-done | bytes 1048600
  16.1 1.0 %copy-done.6 = bf16[1024,512]{1,0:T(8,128)(2,1)} copy-done((bf16[1024,512]{1,0:T(8,128)(2,1)}, bf16[1024,512]{1,0:T(8,128)(2,1)S(1)}, u32[]{:S(2)}) %copy-start.6) | copy-done | bytes 1048600
  17.1 0.7 %copy-done.8 = bf16[16,64,128]{2,1,0:T(8,128)(2,1)} copy-done((bf16[16,64,128]{2,1,0:T(8,128)(2,1)}, bf16[16,64,128]{2,1,0:T(8,128)(2,1)S(1)}, u32[]{:S(2)}) %copy-start.8) | copy-done | bytes 262168
  17.8 0.7 %copy-done.10 = bf16[2,256,256]{2,1,0:T(8,128)(2,1)} copy-done((bf16[2,256,256]{2,1,0:T(8,128)(2,1)}, bf16[2,256,256]{2,1,0:T(8,128)(2,1)S(1)}, u32[]{:S(2)}) %copy-start.10) | copy-done | bytes 262168
  18.5 0.7 %copy-done.12 = bf16[512,256]{1,0:T(8,128)(2,1)} copy-done((bf16[512,256]{1,0:T(8,128)(2,1)}, bf16[512,256]{1,0:T(8,128)(2,1)S(1)}, u32[]{:S(2)}) %copy-start.12) | copy-done | bytes 262168
  19.2 1.3 %collective-permute-start.2 = (bf16[576,128]{1,0:T(8,128)(2,1)}, bf16[576,128]{1,0:T(8,128)(2,1)}, u32[]{:S(2)}, u32[]{:S(2)}) collective-permute-start(bf16[576,128]{1,0:T(8,128)(2,1)} %get-tuple-element.29), channel_id=1, source_target_pairs={{1,2},{2,1},{5,6},{6,5},{9,10},{10,9},{13,14},{14,13},{17,18},{18,... | collective-permute-start | bytes 442376 | tf_op jit(solution)/shard_map/ppermute | solution.py:344
  20.6 1.3 %collective-permute-start.3 = (bf16[576,128]{1,0:T(8,128)(2,1)}, bf16[576,128]{1,0:T(8,128)(2,1)}, u32[]{:S(2)}, u32[]{:S(2)}) collective-permute-start(bf16[576,128]{1,0:T(8,128)(2,1)} %collective-permute-done.1.refs_4_), channel_id=1, source_target_pairs={{2,3},{1,0},{6,7},{5,4},{10,11},{9,8},{14,15},{13,12},{18,19},{17,... | collective-permute-start | bytes 442376 | tf_op jit(solution)/shard_map/ppermute | solution.py:345
  21.9 6.0 %collective-permute-done.3.refs_6_ = bf16[576,128]{1,0:T(8,128)(2,1)} collective-permute-done((bf16[576,128]{1,0:T(8,128)(2,1)}, bf16[576,128]{1,0:T(8,128)(2,1)}, u32[]{:S(2)}, u32[]{:S(2)}) %collective-permute-start.3) | collective-permute-done | bytes 147488 | tf_op jit(solution)/shard_map/ppermute | solution.py:345
  27.9 1.5 %copy-done.1 = bf16[896,1024]{1,0:T(8,128)(2,1)S(1)} copy-done((bf16[896,1024]{1,0:T(8,128)(2,1)S(1)}, bf16[896,1024]{1,0:T(8,128)(2,1)}, u32[]{:S(2)}) %copy-start.1) | copy-done | bytes 1835032
  29.4 0.9 %copy-done.9 = bf16[16,64,128]{2,1,0:T(8,128)(2,1)S(1)} copy-done((bf16[16,64,128]{2,1,0:T(8,128)(2,1)S(1)}, bf16[16,64,128]{2,1,0:T(8,128)(2,1)}, u32[]{:S(2)}) %copy-start.9) | copy-done | bytes 262168
  30.4 2.5 %shard_map.142 = (bf16[1024,64]{1,0:T(8,128)(2,1)S(1)}, bf16[128,256]{1,0:T(8,128)(2,1)S(1)}, bf16[64,128]{1,0:T(8,128)(2,1)S(1)}, bf16[64,128]{1,0:T(8,128)(2,1...) custom-call(s32[16,2]{1,0:T(8,128)S(1)} %copy.15.refs_0_, ...), custom_call_target="tpu_custom_call" | custom-call | flops 134217728 | bytes 2097152 | tf_op jit(solution)/shard_map/pallas_call | solution.py:42
  32.9 0.2 collective-permute-start.4
  33.1 2.3 %collective-permute-start.5 = (bf16[64,128]{1,0:T(8,128)(2,1)S(1)}, bf16[64,128]{1,0:T(8,128)(2,1)S(1)}, u32[]{:S(2)}, u32[]{:S(2)}) collective-permute-start(bf16[64,128]{1,0:T(8,128)(2,1)S(1)} %get-tuple-element.39), channel_id=1, source_target_pairs={{0,24},{4,28},{8,16},{12,20},{16,8},{20,12},{24,0},{28,4},{1,25},{... | collective-permute-start | bytes 49160 | tf_op jit(solution)/shard_map/ppermute | solution.py:423
  35.5 1.4 %collective-permute-start.6 = (bf16[64,128]{1,0:T(8,128)(2,1)S(1)}, bf16[64,128]{1,0:T(8,128)(2,1)S(1)}, u32[]{:S(2)}, u32[]{:S(2)}) collective-permute-start(bf16[64,128]{1,0:T(8,128)(2,1)S(1)} %get-tuple-element.40), channel_id=1, source_target_pairs={{0,20},{4,16},{8,28},{12,24},{16,4},{20,0},{24,12},{28,8},{1,21},{... | collective-permute-start | bytes 49160 | tf_op jit(solution)/shard_map/ppermute | solution.py:423
  36.8 0.5 collective-permute-start.7
  37.3 0.7 %collective-permute-start.8 = (bf16[64,128]{1,0:T(8,128)(2,1)S(1)}, bf16[64,128]{1,0:T(8,128)(2,1)S(1)}, u32[]{:S(2)}, u32[]{:S(2)}) collective-permute-start(bf16[64,128]{1,0:T(8,128)(2,1)S(1)} %get-tuple-element.42), channel_id=1, source_target_pairs={{0,12},{4,8},{8,4},{12,0},{16,28},{20,24},{24,20},{28,16},{1,13},{... | collective-permute-start | bytes 49160 | tf_op jit(solution)/shard_map/ppermute | solution.py:423
  38.1 0.9 %collective-permute-start.9 = (bf16[64,128]{1,0:T(8,128)(2,1)S(1)}, bf16[64,128]{1,0:T(8,128)(2,1)S(1)}, u32[]{:S(2)}, u32[]{:S(2)}) collective-permute-start(bf16[64,128]{1,0:T(8,128)(2,1)S(1)} %get-tuple-element.43), channel_id=1, source_target_pairs={{0,8},{4,12},{8,0},{12,4},{16,24},{20,28},{24,16},{28,20},{1,9},{5... | collective-permute-start | bytes 49160 | tf_op jit(solution)/shard_map/ppermute | solution.py:423
  39.2 1.6 %shard_map.143.refs_0_ = f32[1024,512]{1,0:T(8,128)S(1)} custom-call(bf16[1024,512]{1,0:T(8,128)(2,1)S(1)} %copy-done.7, bf16[1024,64]{1,0:T(8,128)(2,1)S(1)} %get-tuple-element.31.trip_ref, bf16[1024,1024]{1,0:T(8,128)(2,1)S(1)} %get-tuple-element.32.local_ref, bf16[2,64,512]{2,1,0:T(8,128)(2,1)S(1)} %get-tuple-element.33.up_ref.refs_2_), custom_call_target="tpu_custom_call" | custom-call | flops 268435456 | bytes 5242880 | tf_op jit(solution)/shard_map/pallas_call | solution.py:42
  40.9 1.0 %collective-permute-done.9.refs_11_ = bf16[64,128]{1,0:T(8,128)(2,1)S(1)} collective-permute-done((bf16[64,128]{1,0:T(8,128)(2,1)S(1)}, bf16[64,128]{1,0:T(8,128)(2,1)S(1)}, u32[]{:S(2)}, u32[]{:S(2)}) %collective-permute-start.9) | collective-permute-done | bytes 16416 | tf_op jit(solution)/shard_map/ppermute | solution.py:423
  41.9 3.0 %shard_map.144 = (bf16[1024,512]{1,0:T(8,128)(2,1)S(1)}, bf16[128,256]{1,0:T(8,128)(2,1)S(1)}) custom-call(f32[1024,512]{1,0:T(8,128)S(1)} %shard_map.143.refs_0_, bf16[1024,896]{1,0:T(8,128)(2,1)S(1)} %copy-done.3, bf16[2,64,512]{2,1,0:T(8,128)(2,1)S(1)} %get-tuple-element.33.up_ref.refs_2_, bf16[1,2,512,512]{3,2,1,0:T(8,128)(2,1)S(1)} %copy-done.5, ...), custom_call_target="tpu_custom_call" | custom-call | flops 1073741824 | bytes 4194304 | tf_op jit(solution)/shard_map/pallas_call | solution.py:42
  45.0 1.9 %collective-permute-start.12 = (bf16[128,256]{1,0:T(8,128)(2,1)S(1)}, bf16[128,256]{1,0:T(8,128)(2,1)S(1)}, u32[]{:S(2)}, u32[]{:S(2)}) collective-permute-start(bf16[128,256]{1,0:T(8,128)(2,1)S(1)} %get-tuple-element.45.refs_0_), channel_id=1, source_target_pairs={{0,3},{1,2},{2,1},{3,0},{4,7},{5,6},{6,5},{7,4},{8,11},{9,10},{10,... | collective-permute-start | bytes 196616 | tf_op jit(solution)/shard_map/ppermute | solution.py:333
  46.9 1.6 %collective-permute-start.11 = (bf16[128,256]{1,0:T(8,128)(2,1)S(1)}, bf16[128,256]{1,0:T(8,128)(2,1)S(1)}, u32[]{:S(2)}, u32[]{:S(2)}) collective-permute-start(bf16[128,256]{1,0:T(8,128)(2,1)S(1)} %get-tuple-element.45.refs_0_), channel_id=1, source_target_pairs={{0,1},{1,0},{2,3},{3,2},{4,5},{5,4},{6,7},{7,6},{8,9},{9,8},{10,11... | collective-permute-start | bytes 196616 | tf_op jit(solution)/shard_map/ppermute | solution.py:333
  48.5 0.8 %shard_map.145 = (f32[1024,512]{1,0:T(8,128)S(1)}, bf16[1024,256]{1,0:T(8,128)(2,1)S(1)}) custom-call(bf16[1024,512]{1,0:T(8,128)(2,1)S(1)} %get-tuple-element.49.state_ref.refs_7_, bf16[1024,512]{1,0:T(8,128)(2,1)S(1)} %get-tuple-element.48.join_ref.refs_6_, s32[2,1024]{1,0:T(2,128)S(1)} %get-tuple-element.37.refs_5_.index_ref), custom_call_target="tpu_custom_call" | custom-call | flops 536870912 | bytes 4194304 | tf_op jit(solution)/shard_map/pallas_call | solution.py:42
  49.3 3.0 %collective-permute-done.13.refs_3_ = bf16[128,256]{1,0:T(8,128)(2,1)S(1)} collective-permute-done((bf16[128,256]{1,0:T(8,128)(2,1)S(1)}, bf16[128,256]{1,0:T(8,128)(2,1)S(1)}, u32[]{:S(2)}, u32[]{:S(2)}) %collective-permute-start.13) | collective-permute-done | bytes 65568 | tf_op jit(solution)/shard_map/ppermute | solution.py:333
  52.3 0.8 %collective-permute-done.11.refs_1_ = bf16[128,256]{1,0:T(8,128)(2,1)S(1)} collective-permute-done((bf16[128,256]{1,0:T(8,128)(2,1)S(1)}, bf16[128,256]{1,0:T(8,128)(2,1)S(1)}, u32[]{:S(2)}, u32[]{:S(2)}) %collective-permute-start.11) | collective-permute-done | bytes 65568 | tf_op jit(solution)/shard_map/ppermute | solution.py:333
  53.2 2.1 %shard_map.146 = (bf16[1024,512]{1,0:T(8,128)(2,1)}, bf16[32,256]{1,0:T(8,128)(2,1)}) custom-call(bf16[128,256]{1,0:T(8,128)(2,1)S(1)} %get-tuple-element.45.refs_0_, bf16[128,256]{1,0:T(8,128)(2,1)S(1)} %collective-permute-done.11.refs_1_, bf16[128,256]{1,0:T(8,128)(2,1)S(1)} %collective-permute-done.12.refs_2_, ...), custom_call_target="tpu_custom_call" | custom-call | flops 268435456 | bytes 4194304 | tf_op jit(solution)/shard_map/pallas_call | solution.py:42
  (36 shorter events, 0.5 us)
Async XLA Ops:
  0.6 8.7 %copy-start.14 = (s32[1024]{0:T(1024)S(1)}, s32[1024]{0:T(1024)}, u32[]{:S(2)}) copy-start(s32[1024]{0:T(1024)} %param.15) | copy-start | bytes 12292
  3.7 16.9 %collective-permute-start.1 = (bf16[576,128]{1,0:T(8,128)(2,1)S(1)}, bf16[576,128]{1,0:T(8,128)(2,1)}, u32[]{:S(2)}, u32[]{:S(2)}) collective-permute-start(bf16[576,128]{1,0:T(8,128)(2,1)S(1)} %shard_map.140.refs_1_.refs_2_), channel_id=1, source_target_pairs={{0,2},{1,3},{2,0},{3,1},{4,6},{5,7},{6,4},{7,5},{8,10},{9,11},{10,... | collective-permute-start | bytes 442376 | tf_op jit(solution)/shard_map/ppermute | solution.py:342
  7.8 14.2 %collective-permute-start = (bf16[576,128]{1,0:T(8,128)(2,1)S(1)}, bf16[576,128]{1,0:T(8,128)(2,1)}, u32[]{:S(2)}, u32[]{:S(2)}) collective-permute-start(bf16[576,128]{1,0:T(8,128)(2,1)S(1)} %shard_map.140.refs_1_.refs_2_), channel_id=1, source_target_pairs={{0,1},{1,0},{2,3},{3,2},{4,5},{5,4},{6,7},{7,6},{8,9},{9,8},{10,11... | collective-permute-start | bytes 442376 | tf_op jit(solution)/shard_map/ppermute | solution.py:341
  9.3 12.5 %copy-start.15 = (s32[16,2]{0,1:T(2,128)S(1)}, s32[16,2]{0,1:T(2,128)}, u32[]{:S(2)}) copy-start(s32[16,2]{0,1:T(2,128)} %param.17) | copy-start | bytes 388
  12.7 1.2 %copy-start = (bf16[896,1024]{1,0:T(8,128)(2,1)}, bf16[896,1024]{1,0:T(8,128)(2,1)S(1)}, u32[]{:S(2)}) copy-start(bf16[896,1024]{1,0:T(8,128)(2,1)S(1)} %get-tuple-element.30.refs_7_) | copy-start | bytes 5505028
  13.9 1.3 %copy-start.2 = (bf16[1024,896]{1,0:T(8,128)(2,1)}, bf16[1024,896]{1,0:T(8,128)(2,1)S(1)}, u32[]{:S(2)}) copy-start(bf16[1024,896]{1,0:T(8,128)(2,1)S(1)} %get-tuple-element.34.refs_1_) | copy-start | bytes 5505028
  15.2 1.0 %copy-start.4 = (bf16[1,2,512,512]{3,2,1,0:T(8,128)(2,1)}, bf16[1,2,512,512]{3,2,1,0:T(8,128)(2,1)S(1)}, u32[]{:S(2)}) copy-start(bf16[1,2,512,512]{3,2,1,0:T(8,128)(2,1)S(1)} %get-tuple-element.35.refs_3_) | copy-start | bytes 3145732
  16.1 1.0 %copy-start.6 = (bf16[1024,512]{1,0:T(8,128)(2,1)}, bf16[1024,512]{1,0:T(8,128)(2,1)S(1)}, u32[]{:S(2)}) copy-start(bf16[1024,512]{1,0:T(8,128)(2,1)S(1)} %get-tuple-element.27.edges_ref) | copy-start | bytes 3145732
  17.1 0.7 %copy-start.8 = (bf16[16,64,128]{2,1,0:T(8,128)(2,1)}, bf16[16,64,128]{2,1,0:T(8,128)(2,1)S(1)}, u32[]{:S(2)}) copy-start(bf16[16,64,128]{2,1,0:T(8,128)(2,1)S(1)} %get-tuple-element.28.refs_1_) | copy-start | bytes 786436
  17.8 0.7 %copy-start.10 = (bf16[2,256,256]{2,1,0:T(8,128)(2,1)}, bf16[2,256,256]{2,1,0:T(8,128)(2,1)S(1)}, u32[]{:S(2)}) copy-start(bf16[2,256,256]{2,1,0:T(8,128)(2,1)S(1)} %get-tuple-element.47.refs_5_) | copy-start | bytes 786436
  18.5 0.7 %copy-start.12 = (bf16[512,256]{1,0:T(8,128)(2,1)}, bf16[512,256]{1,0:T(8,128)(2,1)S(1)}, u32[]{:S(2)}) copy-start(bf16[512,256]{1,0:T(8,128)(2,1)S(1)} %get-tuple-element.36.refs_4_) | copy-start | bytes 786436
  19.2 2.7 %collective-permute-start.2 = (bf16[576,128]{1,0:T(8,128)(2,1)}, bf16[576,128]{1,0:T(8,128)(2,1)}, u32[]{:S(2)}, u32[]{:S(2)}) collective-permute-start(bf16[576,128]{1,0:T(8,128)(2,1)} %get-tuple-element.29), channel_id=1, source_target_pairs={{1,2},{2,1},{5,6},{6,5},{9,10},{10,9},{13,14},{14,13},{17,18},{18,... | collective-permute-start | bytes 442376 | tf_op jit(solution)/shard_map/ppermute | solution.py:344
  20.6 7.3 %collective-permute-start.3 = (bf16[576,128]{1,0:T(8,128)(2,1)}, bf16[576,128]{1,0:T(8,128)(2,1)}, u32[]{:S(2)}, u32[]{:S(2)}) collective-permute-start(bf16[576,128]{1,0:T(8,128)(2,1)} %collective-permute-done.1.refs_4_), channel_id=1, source_target_pairs={{2,3},{1,0},{6,7},{5,4},{10,11},{9,8},{14,15},{13,12},{18,19},{17,... | collective-permute-start | bytes 442376 | tf_op jit(solution)/shard_map/ppermute | solution.py:345
  27.9 1.5 %copy-start.1 = (bf16[896,1024]{1,0:T(8,128)(2,1)S(1)}, bf16[896,1024]{1,0:T(8,128)(2,1)}, u32[]{:S(2)}) copy-start(bf16[896,1024]{1,0:T(8,128)(2,1)} %copy-done) | copy-start | bytes 5505028
  29.4 0.9 %copy-start.9 = (bf16[16,64,128]{2,1,0:T(8,128)(2,1)S(1)}, bf16[16,64,128]{2,1,0:T(8,128)(2,1)}, u32[]{:S(2)}) copy-start(bf16[16,64,128]{2,1,0:T(8,128)(2,1)} %copy-done.8) | copy-start | bytes 786436
  30.4 8.9 %copy-start.7 = (bf16[1024,512]{1,0:T(8,128)(2,1)S(1)}, bf16[1024,512]{1,0:T(8,128)(2,1)}, u32[]{:S(2)}) copy-start(bf16[1024,512]{1,0:T(8,128)(2,1)} %copy-done.6) | copy-start | bytes 3145732
  32.9 5.2 %collective-permute-start.4 = (bf16[64,128]{1,0:T(8,128)(2,1)S(1)}, bf16[64,128]{1,0:T(8,128)(2,1)S(1)}, u32[]{:S(2)}, u32[]{:S(2)}) collective-permute-start(bf16[64,128]{1,0:T(8,128)(2,1)S(1)} %get-tuple-element.38), channel_id=1, source_target_pairs={{0,28},{4,24},{8,20},{12,16},{16,12},{20,8},{24,4},{28,0},{1,29},{... | collective-permute-start | bytes 49160 | tf_op jit(solution)/shard_map/ppermute | solution.py:423
  33.1 5.8 %collective-permute-start.5 = (bf16[64,128]{1,0:T(8,128)(2,1)S(1)}, bf16[64,128]{1,0:T(8,128)(2,1)S(1)}, u32[]{:S(2)}, u32[]{:S(2)}) collective-permute-start(bf16[64,128]{1,0:T(8,128)(2,1)S(1)} %get-tuple-element.39), channel_id=1, source_target_pairs={{0,24},{4,28},{8,16},{12,20},{16,8},{20,12},{24,0},{28,4},{1,25},{... | collective-permute-start | bytes 49160 | tf_op jit(solution)/shard_map/ppermute | solution.py:423
  35.5 5.3 %collective-permute-start.6 = (bf16[64,128]{1,0:T(8,128)(2,1)S(1)}, bf16[64,128]{1,0:T(8,128)(2,1)S(1)}, u32[]{:S(2)}, u32[]{:S(2)}) collective-permute-start(bf16[64,128]{1,0:T(8,128)(2,1)S(1)} %get-tuple-element.40), channel_id=1, source_target_pairs={{0,20},{4,16},{8,28},{12,24},{16,4},{20,0},{24,12},{28,8},{1,21},{... | collective-permute-start | bytes 49160 | tf_op jit(solution)/shard_map/ppermute | solution.py:423
  36.8 4.0 %collective-permute-start.7 = (bf16[64,128]{1,0:T(8,128)(2,1)S(1)}, bf16[64,128]{1,0:T(8,128)(2,1)S(1)}, u32[]{:S(2)}, u32[]{:S(2)}) collective-permute-start(bf16[64,128]{1,0:T(8,128)(2,1)S(1)} %get-tuple-element.41), channel_id=1, source_target_pairs={{0,16},{4,20},{8,24},{12,28},{16,0},{20,4},{24,8},{28,12},{1,17},{... | collective-permute-start | bytes 49160 | tf_op jit(solution)/shard_map/ppermute | solution.py:423
  37.3 3.5 %collective-permute-start.8 = (bf16[64,128]{1,0:T(8,128)(2,1)S(1)}, bf16[64,128]{1,0:T(8,128)(2,1)S(1)}, u32[]{:S(2)}, u32[]{:S(2)}) collective-permute-start(bf16[64,128]{1,0:T(8,128)(2,1)S(1)} %get-tuple-element.42), channel_id=1, source_target_pairs={{0,12},{4,8},{8,4},{12,0},{16,28},{20,24},{24,20},{28,16},{1,13},{... | collective-permute-start | bytes 49160 | tf_op jit(solution)/shard_map/ppermute | solution.py:423
  38.1 3.8 %collective-permute-start.9 = (bf16[64,128]{1,0:T(8,128)(2,1)S(1)}, bf16[64,128]{1,0:T(8,128)(2,1)S(1)}, u32[]{:S(2)}, u32[]{:S(2)}) collective-permute-start(bf16[64,128]{1,0:T(8,128)(2,1)S(1)} %get-tuple-element.43), channel_id=1, source_target_pairs={{0,8},{4,12},{8,0},{12,4},{16,24},{20,28},{24,16},{28,20},{1,9},{5... | collective-permute-start | bytes 49160 | tf_op jit(solution)/shard_map/ppermute | solution.py:423
  39.0 2.9 %collective-permute-start.10 = (bf16[64,128]{1,0:T(8,128)(2,1)S(1)}, bf16[64,128]{1,0:T(8,128)(2,1)S(1)}, u32[]{:S(2)}, u32[]{:S(2)}) collective-permute-start(bf16[64,128]{1,0:T(8,128)(2,1)S(1)} %get-tuple-element.44), channel_id=1, source_target_pairs={{0,4},{4,0},{8,12},{12,8},{16,20},{20,16},{24,28},{28,24},{1,5},{5... | collective-permute-start | bytes 49160 | tf_op jit(solution)/shard_map/ppermute | solution.py:423
  39.2 2.7 %copy-start.3 = (bf16[1024,896]{1,0:T(8,128)(2,1)S(1)}, bf16[1024,896]{1,0:T(8,128)(2,1)}, u32[]{:S(2)}) copy-start(bf16[1024,896]{1,0:T(8,128)(2,1)} %copy-done.2) | copy-start | bytes 5505028
  39.2 2.7 %copy-start.5 = (bf16[1,2,512,512]{3,2,1,0:T(8,128)(2,1)S(1)}, bf16[1,2,512,512]{3,2,1,0:T(8,128)(2,1)}, u32[]{:S(2)}) copy-start(bf16[1,2,512,512]{3,2,1,0:T(8,128)(2,1)} %copy-done.4) | copy-start | bytes 3145732
  39.2 2.7 %copy-start.13 = (bf16[512,256]{1,0:T(8,128)(2,1)S(1)}, bf16[512,256]{1,0:T(8,128)(2,1)}, u32[]{:S(2)}) copy-start(bf16[512,256]{1,0:T(8,128)(2,1)} %copy-done.12) | copy-start | bytes 786436
  45.0 8.2 %copy-start.11 = (bf16[2,256,256]{2,1,0:T(8,128)(2,1)S(1)}, bf16[2,256,256]{2,1,0:T(8,128)(2,1)}, u32[]{:S(2)}) copy-start(bf16[2,256,256]{2,1,0:T(8,128)(2,1)} %copy-done.10) | copy-start | bytes 786436
  45.0 7.4 %collective-permute-start.13 = (bf16[128,256]{1,0:T(8,128)(2,1)S(1)}, bf16[128,256]{1,0:T(8,128)(2,1)S(1)}, u32[]{:S(2)}, u32[]{:S(2)}) collective-permute-start(bf16[128,256]{1,0:T(8,128)(2,1)S(1)} %get-tuple-element.45.refs_0_), channel_id=1, source_target_pairs={{0,2},{1,3},{2,0},{3,1},{4,6},{5,7},{6,4},{7,5},{8,10},{9,11},{10,... | collective-permute-start | bytes 196616 | tf_op jit(solution)/shard_map/ppermute | solution.py:333
  45.0 7.3 %collective-permute-start.12 = (bf16[128,256]{1,0:T(8,128)(2,1)S(1)}, bf16[128,256]{1,0:T(8,128)(2,1)S(1)}, u32[]{:S(2)}, u32[]{:S(2)}) collective-permute-start(bf16[128,256]{1,0:T(8,128)(2,1)S(1)} %get-tuple-element.45.refs_0_), channel_id=1, source_target_pairs={{0,3},{1,2},{2,1},{3,0},{4,7},{5,6},{6,5},{7,4},{8,11},{9,10},{10,... | collective-permute-start | bytes 196616 | tf_op jit(solution)/shard_map/ppermute | solution.py:333
  46.9 6.2 %collective-permute-start.11 = (bf16[128,256]{1,0:T(8,128)(2,1)S(1)}, bf16[128,256]{1,0:T(8,128)(2,1)S(1)}, u32[]{:S(2)}, u32[]{:S(2)}) collective-permute-start(bf16[128,256]{1,0:T(8,128)(2,1)S(1)} %get-tuple-element.45.refs_0_), channel_id=1, source_target_pairs={{0,1},{1,0},{2,3},{3,2},{4,5},{5,4},{6,7},{7,6},{8,9},{9,8},{10,11... | collective-permute-start | bytes 196616 | tf_op jit(solution)/shard_map/ppermute | solution.py:333
where the time goes:
time: 55.5 us; the launch traced here: 55.3 us
  starting transfers between devices  18.1 us (33%)
  Pallas kernels  16.3 us (29%)
  waiting for transfers between devices  10.9 us (20%)
  local copies, waits for them, and re-layouts  9.11 us (16%)
  between operations  0.79 us (1%)
    pallas_call x7, Pallas kernels, call(): pl.pallas_call(kernel, out_shape=outs, in_specs=[pl.BlockSpec(memory_spac...  16.3 us
    unnamed x33, local copies, waits for them, and re-layouts  9.11 us
    ppermute x7, starting transfers between devices, body(): lax.ppermute(block, 'dom', [(at, at ^ partners - place) for at in range(d...  6.32 us
    ppermute x1, waiting for transfers between devices, by_relay(): relayed = lax.ppermute(far, 'edge', [(2, 3), (1, 0)])  5.95 us
    ppermute x1, starting transfers between devices, by_relay(): far = lax.ppermute(value, 'edge', [(at, at ^ 2) for at in range(4)])  4.1 us
    ppermute x3, waiting for transfers between devices, from_others(): lax.ppermute(value, 'edge', [(at, at ^ by) for at in range(shards)])  3.86 us
    ppermute x3, starting transfers between devices, from_others(): lax.ppermute(value, 'edge', [(at, at ^ by) for at in range(shards)])  3.55 us
    ppermute x1, starting transfers between devices, by_relay(): near = lax.ppermute(value, 'edge', [(at, at ^ 1) for at in range(4)])  1.58 us
  transfers between devices with their start and end apart: 14, of which 4 were waited for; matrix products, arithmetic and copies ran while one was open for 0% of the time, Pallas kernels for 10%

commit v1 on v0

--- a/solution.py
+++ b/solution.py
@@ -341,8 +341,8 @@
     near = lax.ppermute(value, "edge", [(at, at ^ 1) for at in range(4)])
     far = lax.ppermute(value, "edge", [(at, at ^ 2) for at in range(4)])
     others = between(value)
-    middle = lax.ppermute(others[0], "edge", [(1, 2), (2, 1)])
-    relayed = lax.ppermute(far, "edge", [(2, 3), (1, 0)])
+    middle = lax.ppermute(others[0], "edge", [(0, 0), (1, 2), (2, 1), (3, 3)])
+    relayed = lax.ppermute(far, "edge", [(at, at ^ 1) for at in range(4)])
     return [value, near, far, middle, relayed], others
 
 

time: 55.5 us -> 55.6 us (level)
    ppermute x2, waiting for transfers between devices: 5.96 us -> 5.31 us  [the longest x1 5.31 us: by_relay(): relayed = lax.ppermute(far, 'edge', [(at, at ^ 1) for at in range(4)])]
where the time goes in v1:
time: 55.6 us; the launch traced here: 55.3 us
  starting transfers between devices  18.4 us (33%)
  Pallas kernels  16.3 us (29%)
  waiting for transfers between devices  10.6 us (19%)
  local copies, waits for them, and re-layouts  9.11 us (16%)
  between operations  0.76 us (1%)
    pallas_call x7, Pallas kernels, call(): pl.pallas_call(kernel, out_shape=outs, in_specs=[pl.BlockSpec(memory_spac...  16.3 us
    unnamed x33, local copies, waits for them, and re-layouts  9.11 us
    ppermute x7, starting transfers between devices, body(): lax.ppermute(block, 'dom', [(at, at ^ partners - place) for at in range(d...  6.32 us
    ppermute x1, waiting for transfers between devices, by_relay(): relayed = lax.ppermute(far, 'edge', [(at, at ^ 1) for at in range(4)])  5.31 us
    ppermute x3, waiting for transfers between devices, from_others(): lax.ppermute(value, 'edge', [(at, at ^ by) for at in range(shards)])  4.26 us
    ppermute x1, starting transfers between devices, by_relay(): far = lax.ppermute(value, 'edge', [(at, at ^ 2) for at in range(4)])  4.1 us
    ppermute x3, starting transfers between devices, from_others(): lax.ppermute(value, 'edge', [(at, at ^ by) for at in range(shards)])  3.55 us
    ppermute x1, starting transfers between devices, by_relay(): middle = lax.ppermute(others[0], 'edge', [(0, 0), (1, 2), (2, 1), (3, 3)])  2.82 us
  transfers between devices with their start and end apart: 14, of which 4 were waited for; matrix products, arithmetic and copies ran while one was open for 0% of the time, Pallas kernels for 10%

profile of v1, /device:TPU:0, one launch (start us, length us, event | category | flops | bytes accessed | tf_op | source)
XLA Modules:
  0.0 55.3 jit_solution(13929757345375181882)
XLA Ops:
  0.6 3.0 %shard_map.140.refs_1_.refs_2_ = bf16[576,128]{1,0:T(8,128)(2,1)S(1)} custom-call(bf16[1024,512]{1,0:T(8,128)(2,1)} %refs_2_.1, bf16[512,512]{1,0:T(8,128)(2,1)} %weight_hbm.1, bf16[64,512]{1,0:T(8,128)(2,1)} %down_hbm.1, bf16[32,256]{1,0:T(8,128)(2,1)} %atoms_hbm.1), custom_call_target="tpu_custom_call" | custom-call | flops 603979776 | bytes 1572864 | tf_op jit(solution)/shard_map/pallas_call | solution.py:42
  3.7 4.1 %collective-permute-start.1 = (bf16[576,128]{1,0:T(8,128)(2,1)S(1)}, bf16[576,128]{1,0:T(8,128)(2,1)}, u32[]{:S(2)}, u32[]{:S(2)}) collective-permute-start(bf16[576,128]{1,0:T(8,128)(2,1)S(1)} %shard_map.140.refs_1_.refs_2_), channel_id=1, source_target_pairs={{0,2},{1,3},{2,0},{3,1},{4,6},{5,7},{6,4},{7,5},{8,10},{9,11},{10,... | collective-permute-start | bytes 442376 | tf_op jit(solution)/shard_map/ppermute | solution.py:342
  7.8 1.6 %collective-permute-start = (bf16[576,128]{1,0:T(8,128)(2,1)S(1)}, bf16[576,128]{1,0:T(8,128)(2,1)}, u32[]{:S(2)}, u32[]{:S(2)}) collective-permute-start(bf16[576,128]{1,0:T(8,128)(2,1)S(1)} %shard_map.140.refs_1_.refs_2_), channel_id=1, source_target_pairs={{0,1},{1,0},{2,3},{3,2},{4,5},{5,4},{6,7},{7,6},{8,9},{9,8},{10,11... | collective-permute-start | bytes 442376 | tf_op jit(solution)/shard_map/ppermute | solution.py:341
  9.3 3.3 %shard_map.141 = (bf16[576,128]{1,0:T(8,128)(2,1)}, bf16[896,1024]{1,0:T(8,128)(2,1)S(1)}, bf16[1024,896]{1,0:T(8,128)(2,1)S(1)}, bf16[1024,1024]{1,0:T(8,128)(2...) custom-call(s32[1,1024]{1,0:T(1,128)S(1)} %bitcast.1, ...), custom_call_target="tpu_custom_call" | custom-call | flops 41943040 | bytes 6291456 | tf_op jit(solution)/shard_map/pallas_call | solution.py:42
  12.7 1.2 %copy-done = bf16[896,1024]{1,0:T(8,128)(2,1)} copy-done((bf16[896,1024]{1,0:T(8,128)(2,1)}, bf16[896,1024]{1,0:T(8,128)(2,1)S(1)}, u32[]{:S(2)}) %copy-start) | copy-done | bytes 1835032
  13.9 1.3 %copy-done.2 = bf16[1024,896]{1,0:T(8,128)(2,1)} copy-done((bf16[1024,896]{1,0:T(8,128)(2,1)}, bf16[1024,896]{1,0:T(8,128)(2,1)S(1)}, u32[]{:S(2)}) %copy-start.2) | copy-done | bytes 1835032
  15.2 1.0 %copy-done.4 = bf16[1,2,512,512]{3,2,1,0:T(8,128)(2,1)} copy-done((bf16[1,2,512,512]{3,2,1,0:T(8,128)(2,1)}, bf16[1,2,512,512]{3,2,1,0:T(8,128)(2,1)S(1)}, u32[]{:S(2)}) %copy-start.4) | copy-done | bytes 1048600
  16.1 1.0 %copy-done.6 = bf16[1024,512]{1,0:T(8,128)(2,1)} copy-done((bf16[1024,512]{1,0:T(8,128)(2,1)}, bf16[1024,512]{1,0:T(8,128)(2,1)S(1)}, u32[]{:S(2)}) %copy-start.6) | copy-done | bytes 1048600
  17.1 0.7 %copy-done.8 = bf16[16,64,128]{2,1,0:T(8,128)(2,1)} copy-done((bf16[16,64,128]{2,1,0:T(8,128)(2,1)}, bf16[16,64,128]{2,1,0:T(8,128)(2,1)S(1)}, u32[]{:S(2)}) %copy-start.8) | copy-done | bytes 262168
  17.8 0.7 %copy-done.10 = bf16[2,256,256]{2,1,0:T(8,128)(2,1)} copy-done((bf16[2,256,256]{2,1,0:T(8,128)(2,1)}, bf16[2,256,256]{2,1,0:T(8,128)(2,1)S(1)}, u32[]{:S(2)}) %copy-start.10) | copy-done | bytes 262168
  18.5 0.7 %copy-done.12 = bf16[512,256]{1,0:T(8,128)(2,1)} copy-done((bf16[512,256]{1,0:T(8,128)(2,1)}, bf16[512,256]{1,0:T(8,128)(2,1)S(1)}, u32[]{:S(2)}) %copy-start.12) | copy-done | bytes 262168
  19.2 2.8 %collective-permute-start.2 = (bf16[576,128]{1,0:T(8,128)(2,1)}, bf16[576,128]{1,0:T(8,128)(2,1)}, u32[]{:S(2)}, u32[]{:S(2)}) collective-permute-start(bf16[576,128]{1,0:T(8,128)(2,1)} %get-tuple-element.29), channel_id=1, source_target_pairs={{0,0},{1,2},{2,1},{3,3},{4,4},{5,6},{6,5},{7,7},{8,8},{9,10},{10,9... | collective-permute-start | bytes 442376 | tf_op jit(solution)/shard_map/ppermute | solution.py:344
  22.2 5.3 %collective-permute-done.3.refs_6_ = bf16[576,128]{1,0:T(8,128)(2,1)} collective-permute-done((bf16[576,128]{1,0:T(8,128)(2,1)}, bf16[576,128]{1,0:T(8,128)(2,1)}, u32[]{:S(2)}, u32[]{:S(2)}) %collective-permute-start.3) | collective-permute-done | bytes 147488 | tf_op jit(solution)/shard_map/ppermute | solution.py:345
  27.5 1.5 %copy-done.1 = bf16[896,1024]{1,0:T(8,128)(2,1)S(1)} copy-done((bf16[896,1024]{1,0:T(8,128)(2,1)S(1)}, bf16[896,1024]{1,0:T(8,128)(2,1)}, u32[]{:S(2)}) %copy-start.1) | copy-done | bytes 1835032
  29.0 0.9 %copy-done.9 = bf16[16,64,128]{2,1,0:T(8,128)(2,1)S(1)} copy-done((bf16[16,64,128]{2,1,0:T(8,128)(2,1)S(1)}, bf16[16,64,128]{2,1,0:T(8,128)(2,1)}, u32[]{:S(2)}) %copy-start.9) | copy-done | bytes 262168
  30.0 2.5 %shard_map.142 = (bf16[1024,64]{1,0:T(8,128)(2,1)S(1)}, bf16[128,256]{1,0:T(8,128)(2,1)S(1)}, bf16[64,128]{1,0:T(8,128)(2,1)S(1)}, bf16[64,128]{1,0:T(8,128)(2,1...) custom-call(s32[16,2]{1,0:T(8,128)S(1)} %copy.15.refs_0_, ...), custom_call_target="tpu_custom_call" | custom-call | flops 134217728 | bytes 2097152 | tf_op jit(solution)/shard_map/pallas_call | solution.py:42
  32.5 0.2 collective-permute-start.4
  32.8 2.3 %collective-permute-start.5 = (bf16[64,128]{1,0:T(8,128)(2,1)S(1)}, bf16[64,128]{1,0:T(8,128)(2,1)S(1)}, u32[]{:S(2)}, u32[]{:S(2)}) collective-permute-start(bf16[64,128]{1,0:T(8,128)(2,1)S(1)} %get-tuple-element.39), channel_id=1, source_target_pairs={{0,24},{4,28},{8,16},{12,20},{16,8},{20,12},{24,0},{28,4},{1,25},{... | collective-permute-start | bytes 49160 | tf_op jit(solution)/shard_map/ppermute | solution.py:423
  35.1 1.4 %collective-permute-start.6 = (bf16[64,128]{1,0:T(8,128)(2,1)S(1)}, bf16[64,128]{1,0:T(8,128)(2,1)S(1)}, u32[]{:S(2)}, u32[]{:S(2)}) collective-permute-start(bf16[64,128]{1,0:T(8,128)(2,1)S(1)} %get-tuple-element.40), channel_id=1, source_target_pairs={{0,20},{4,16},{8,28},{12,24},{16,4},{20,0},{24,12},{28,8},{1,21},{... | collective-permute-start | bytes 49160 | tf_op jit(solution)/shard_map/ppermute | solution.py:423
  36.5 0.5 collective-permute-start.7
  37.0 0.7 %collective-permute-start.8 = (bf16[64,128]{1,0:T(8,128)(2,1)S(1)}, bf16[64,128]{1,0:T(8,128)(2,1)S(1)}, u32[]{:S(2)}, u32[]{:S(2)}) collective-permute-start(bf16[64,128]{1,0:T(8,128)(2,1)S(1)} %get-tuple-element.42), channel_id=1, source_target_pairs={{0,12},{4,8},{8,4},{12,0},{16,28},{20,24},{24,20},{28,16},{1,13},{... | collective-permute-start | bytes 49160 | tf_op jit(solution)/shard_map/ppermute | solution.py:423
  37.7 0.9 %collective-permute-start.9 = (bf16[64,128]{1,0:T(8,128)(2,1)S(1)}, bf16[64,128]{1,0:T(8,128)(2,1)S(1)}, u32[]{:S(2)}, u32[]{:S(2)}) collective-permute-start(bf16[64,128]{1,0:T(8,128)(2,1)S(1)} %get-tuple-element.43), channel_id=1, source_target_pairs={{0,8},{4,12},{8,0},{12,4},{16,24},{20,28},{24,16},{28,20},{1,9},{5... | collective-permute-start | bytes 49160 | tf_op jit(solution)/shard_map/ppermute | solution.py:423
  38.9 1.6 %shard_map.143.refs_0_ = f32[1024,512]{1,0:T(8,128)S(1)} custom-call(bf16[1024,512]{1,0:T(8,128)(2,1)S(1)} %copy-done.7, bf16[1024,64]{1,0:T(8,128)(2,1)S(1)} %get-tuple-element.31.trip_ref, bf16[1024,1024]{1,0:T(8,128)(2,1)S(1)} %get-tuple-element.32.local_ref, bf16[2,64,512]{2,1,0:T(8,128)(2,1)S(1)} %get-tuple-element.33.up_ref.refs_2_), custom_call_target="tpu_custom_call" | custom-call | flops 268435456 | bytes 5242880 | tf_op jit(solution)/shard_map/pallas_call | solution.py:42
  40.5 1.0 %collective-permute-done.9.refs_11_ = bf16[64,128]{1,0:T(8,128)(2,1)S(1)} collective-permute-done((bf16[64,128]{1,0:T(8,128)(2,1)S(1)}, bf16[64,128]{1,0:T(8,128)(2,1)S(1)}, u32[]{:S(2)}, u32[]{:S(2)}) %collective-permute-start.9) | collective-permute-done | bytes 16416 | tf_op jit(solution)/shard_map/ppermute | solution.py:423
  41.6 3.0 %shard_map.144 = (bf16[1024,512]{1,0:T(8,128)(2,1)S(1)}, bf16[128,256]{1,0:T(8,128)(2,1)S(1)}) custom-call(f32[1024,512]{1,0:T(8,128)S(1)} %shard_map.143.refs_0_, bf16[1024,896]{1,0:T(8,128)(2,1)S(1)} %copy-done.3, bf16[2,64,512]{2,1,0:T(8,128)(2,1)S(1)} %get-tuple-element.33.up_ref.refs_2_, bf16[1,2,512,512]{3,2,1,0:T(8,128)(2,1)S(1)} %copy-done.5, ...), custom_call_target="tpu_custom_call" | custom-call | flops 1073741824 | bytes 4194304 | tf_op jit(solution)/shard_map/pallas_call | solution.py:42
  44.6 1.1 %collective-permute-start.13 = (bf16[128,256]{1,0:T(8,128)(2,1)S(1)}, bf16[128,256]{1,0:T(8,128)(2,1)S(1)}, u32[]{:S(2)}, u32[]{:S(2)}) collective-permute-start(bf16[128,256]{1,0:T(8,128)(2,1)S(1)} %get-tuple-element.45.refs_0_), channel_id=1, source_target_pairs={{0,2},{1,3},{2,0},{3,1},{4,6},{5,7},{6,4},{7,5},{8,10},{9,11},{10,... | collective-permute-start | bytes 196616 | tf_op jit(solution)/shard_map/ppermute | solution.py:333
  45.7 1.5 %collective-permute-start.12 = (bf16[128,256]{1,0:T(8,128)(2,1)S(1)}, bf16[128,256]{1,0:T(8,128)(2,1)S(1)}, u32[]{:S(2)}, u32[]{:S(2)}) collective-permute-start(bf16[128,256]{1,0:T(8,128)(2,1)S(1)} %get-tuple-element.45.refs_0_), channel_id=1, source_target_pairs={{0,3},{1,2},{2,1},{3,0},{4,7},{5,6},{6,5},{7,4},{8,11},{9,10},{10,... | collective-permute-start | bytes 196616 | tf_op jit(solution)/shard_map/ppermute | solution.py:333
  47.2 1.0 %collective-permute-start.11 = (bf16[128,256]{1,0:T(8,128)(2,1)S(1)}, bf16[128,256]{1,0:T(8,128)(2,1)S(1)}, u32[]{:S(2)}, u32[]{:S(2)}) collective-permute-start(bf16[128,256]{1,0:T(8,128)(2,1)S(1)} %get-tuple-element.45.refs_0_), channel_id=1, source_target_pairs={{0,1},{1,0},{2,3},{3,2},{4,5},{5,4},{6,7},{7,6},{8,9},{9,8},{10,11... | collective-permute-start | bytes 196616 | tf_op jit(solution)/shard_map/ppermute | solution.py:333
  48.1 0.8 %shard_map.145 = (f32[1024,512]{1,0:T(8,128)S(1)}, bf16[1024,256]{1,0:T(8,128)(2,1)S(1)}) custom-call(bf16[1024,512]{1,0:T(8,128)(2,1)S(1)} %get-tuple-element.49.state_ref.refs_7_, bf16[1024,512]{1,0:T(8,128)(2,1)S(1)} %get-tuple-element.48.join_ref.refs_6_, s32[2,1024]{1,0:T(2,128)S(1)} %get-tuple-element.37.refs_5_.index_ref), custom_call_target="tpu_custom_call" | custom-call | flops 536870912 | bytes 4194304 | tf_op jit(solution)/shard_map/pallas_call | solution.py:42
  48.9 3.4 %collective-permute-done.13.refs_3_ = bf16[128,256]{1,0:T(8,128)(2,1)S(1)} collective-permute-done((bf16[128,256]{1,0:T(8,128)(2,1)S(1)}, bf16[128,256]{1,0:T(8,128)(2,1)S(1)}, u32[]{:S(2)}, u32[]{:S(2)}) %collective-permute-start.13) | collective-permute-done | bytes 65568 | tf_op jit(solution)/shard_map/ppermute | solution.py:333
  52.3 0.9 %collective-permute-done.11.refs_1_ = bf16[128,256]{1,0:T(8,128)(2,1)S(1)} collective-permute-done((bf16[128,256]{1,0:T(8,128)(2,1)S(1)}, bf16[128,256]{1,0:T(8,128)(2,1)S(1)}, u32[]{:S(2)}, u32[]{:S(2)}) %collective-permute-start.11) | collective-permute-done | bytes 65568 | tf_op jit(solution)/shard_map/ppermute | solution.py:333
  53.2 2.1 %shard_map.146 = (bf16[1024,512]{1,0:T(8,128)(2,1)}, bf16[32,256]{1,0:T(8,128)(2,1)}) custom-call(bf16[128,256]{1,0:T(8,128)(2,1)S(1)} %get-tuple-element.45.refs_0_, bf16[128,256]{1,0:T(8,128)(2,1)S(1)} %collective-permute-done.11.refs_1_, bf16[128,256]{1,0:T(8,128)(2,1)S(1)} %collective-permute-done.12.refs_2_, ...), custom_call_target="tpu_custom_call" | custom-call | flops 268435456 | bytes 4194304 | tf_op jit(solution)/shard_map/pallas_call | solution.py:42
  (36 shorter events, 0.4 us)
Async XLA Ops:
  0.6 8.7 %copy-start.14 = (s32[1024]{0:T(1024)S(1)}, s32[1024]{0:T(1024)}, u32[]{:S(2)}) copy-start(s32[1024]{0:T(1024)} %param.15) | copy-start | bytes 12292
  3.7 18.4 %collective-permute-start.1 = (bf16[576,128]{1,0:T(8,128)(2,1)S(1)}, bf16[576,128]{1,0:T(8,128)(2,1)}, u32[]{:S(2)}, u32[]{:S(2)}) collective-permute-start(bf16[576,128]{1,0:T(8,128)(2,1)S(1)} %shard_map.140.refs_1_.refs_2_), channel_id=1, source_target_pairs={{0,2},{1,3},{2,0},{3,1},{4,6},{5,7},{6,4},{7,5},{8,10},{9,11},{10,... | collective-permute-start | bytes 442376 | tf_op jit(solution)/shard_map/ppermute | solution.py:342
  7.8 14.5 %collective-permute-start = (bf16[576,128]{1,0:T(8,128)(2,1)S(1)}, bf16[576,128]{1,0:T(8,128)(2,1)}, u32[]{:S(2)}, u32[]{:S(2)}) collective-permute-start(bf16[576,128]{1,0:T(8,128)(2,1)S(1)} %shard_map.140.refs_1_.refs_2_), channel_id=1, source_target_pairs={{0,1},{1,0},{2,3},{3,2},{4,5},{5,4},{6,7},{7,6},{8,9},{9,8},{10,11... | collective-permute-start | bytes 442376 | tf_op jit(solution)/shard_map/ppermute | solution.py:341
  9.3 12.8 %copy-start.15 = (s32[16,2]{0,1:T(2,128)S(1)}, s32[16,2]{0,1:T(2,128)}, u32[]{:S(2)}) copy-start(s32[16,2]{0,1:T(2,128)} %param.17) | copy-start | bytes 388
  12.7 1.2 %copy-start = (bf16[896,1024]{1,0:T(8,128)(2,1)}, bf16[896,1024]{1,0:T(8,128)(2,1)S(1)}, u32[]{:S(2)}) copy-start(bf16[896,1024]{1,0:T(8,128)(2,1)S(1)} %get-tuple-element.30.refs_7_) | copy-start | bytes 5505028
  13.9 1.3 %copy-start.2 = (bf16[1024,896]{1,0:T(8,128)(2,1)}, bf16[1024,896]{1,0:T(8,128)(2,1)S(1)}, u32[]{:S(2)}) copy-start(bf16[1024,896]{1,0:T(8,128)(2,1)S(1)} %get-tuple-element.34.refs_1_) | copy-start | bytes 5505028
  15.2 1.0 %copy-start.4 = (bf16[1,2,512,512]{3,2,1,0:T(8,128)(2,1)}, bf16[1,2,512,512]{3,2,1,0:T(8,128)(2,1)S(1)}, u32[]{:S(2)}) copy-start(bf16[1,2,512,512]{3,2,1,0:T(8,128)(2,1)S(1)} %get-tuple-element.35.refs_3_) | copy-start | bytes 3145732
  16.1 1.0 %copy-start.6 = (bf16[1024,512]{1,0:T(8,128)(2,1)}, bf16[1024,512]{1,0:T(8,128)(2,1)S(1)}, u32[]{:S(2)}) copy-start(bf16[1024,512]{1,0:T(8,128)(2,1)S(1)} %get-tuple-element.27.edges_ref) | copy-start | bytes 3145732
  17.1 0.7 %copy-start.8 = (bf16[16,64,128]{2,1,0:T(8,128)(2,1)}, bf16[16,64,128]{2,1,0:T(8,128)(2,1)S(1)}, u32[]{:S(2)}) copy-start(bf16[16,64,128]{2,1,0:T(8,128)(2,1)S(1)} %get-tuple-element.28.refs_1_) | copy-start | bytes 786436
  17.8 0.7 %copy-start.10 = (bf16[2,256,256]{2,1,0:T(8,128)(2,1)}, bf16[2,256,256]{2,1,0:T(8,128)(2,1)S(1)}, u32[]{:S(2)}) copy-start(bf16[2,256,256]{2,1,0:T(8,128)(2,1)S(1)} %get-tuple-element.47.refs_5_) | copy-start | bytes 786436
  18.5 0.7 %copy-start.12 = (bf16[512,256]{1,0:T(8,128)(2,1)}, bf16[512,256]{1,0:T(8,128)(2,1)S(1)}, u32[]{:S(2)}) copy-start(bf16[512,256]{1,0:T(8,128)(2,1)S(1)} %get-tuple-element.36.refs_4_) | copy-start | bytes 786436
  19.2 3.0 %collective-permute-start.2 = (bf16[576,128]{1,0:T(8,128)(2,1)}, bf16[576,128]{1,0:T(8,128)(2,1)}, u32[]{:S(2)}, u32[]{:S(2)}) collective-permute-start(bf16[576,128]{1,0:T(8,128)(2,1)} %get-tuple-element.29), channel_id=1, source_target_pairs={{0,0},{1,2},{2,1},{3,3},{4,4},{5,6},{6,5},{7,7},{8,8},{9,10},{10,9... | collective-permute-start | bytes 442376 | tf_op jit(solution)/shard_map/ppermute | solution.py:344
  22.1 5.5 %collective-permute-start.3 = (bf16[576,128]{1,0:T(8,128)(2,1)}, bf16[576,128]{1,0:T(8,128)(2,1)}, u32[]{:S(2)}, u32[]{:S(2)}) collective-permute-start(bf16[576,128]{1,0:T(8,128)(2,1)} %collective-permute-done.1.refs_4_), channel_id=1, source_target_pairs={{0,1},{1,0},{2,3},{3,2},{4,5},{5,4},{6,7},{7,6},{8,9},{9,8},{10,11... | collective-permute-start | bytes 442376 | tf_op jit(solution)/shard_map/ppermute | solution.py:345
  27.5 1.5 %copy-start.1 = (bf16[896,1024]{1,0:T(8,128)(2,1)S(1)}, bf16[896,1024]{1,0:T(8,128)(2,1)}, u32[]{:S(2)}) copy-start(bf16[896,1024]{1,0:T(8,128)(2,1)} %copy-done) | copy-start | bytes 5505028
  29.0 0.9 %copy-start.9 = (bf16[16,64,128]{2,1,0:T(8,128)(2,1)S(1)}, bf16[16,64,128]{2,1,0:T(8,128)(2,1)}, u32[]{:S(2)}) copy-start(bf16[16,64,128]{2,1,0:T(8,128)(2,1)} %copy-done.8) | copy-start | bytes 786436
  30.0 8.9 %copy-start.7 = (bf16[1024,512]{1,0:T(8,128)(2,1)S(1)}, bf16[1024,512]{1,0:T(8,128)(2,1)}, u32[]{:S(2)}) copy-start(bf16[1024,512]{1,0:T(8,128)(2,1)} %copy-done.6) | copy-start | bytes 3145732
  32.5 5.2 %collective-permute-start.4 = (bf16[64,128]{1,0:T(8,128)(2,1)S(1)}, bf16[64,128]{1,0:T(8,128)(2,1)S(1)}, u32[]{:S(2)}, u32[]{:S(2)}) collective-permute-start(bf16[64,128]{1,0:T(8,128)(2,1)S(1)} %get-tuple-element.38), channel_id=1, source_target_pairs={{0,28},{4,24},{8,20},{12,16},{16,12},{20,8},{24,4},{28,0},{1,29},{... | collective-permute-start | bytes 49160 | tf_op jit(solution)/shard_map/ppermute | solution.py:423
  32.8 5.8 %collective-permute-start.5 = (bf16[64,128]{1,0:T(8,128)(2,1)S(1)}, bf16[64,128]{1,0:T(8,128)(2,1)S(1)}, u32[]{:S(2)}, u32[]{:S(2)}) collective-permute-start(bf16[64,128]{1,0:T(8,128)(2,1)S(1)} %get-tuple-element.39), channel_id=1, source_target_pairs={{0,24},{4,28},{8,16},{12,20},{16,8},{20,12},{24,0},{28,4},{1,25},{... | collective-permute-start | bytes 49160 | tf_op jit(solution)/shard_map/ppermute | solution.py:423
  35.1 5.3 %collective-permute-start.6 = (bf16[64,128]{1,0:T(8,128)(2,1)S(1)}, bf16[64,128]{1,0:T(8,128)(2,1)S(1)}, u32[]{:S(2)}, u32[]{:S(2)}) collective-permute-start(bf16[64,128]{1,0:T(8,128)(2,1)S(1)} %get-tuple-element.40), channel_id=1, source_target_pairs={{0,20},{4,16},{8,28},{12,24},{16,4},{20,0},{24,12},{28,8},{1,21},{... | collective-permute-start | bytes 49160 | tf_op jit(solution)/shard_map/ppermute | solution.py:423
  36.5 4.0 %collective-permute-start.7 = (bf16[64,128]{1,0:T(8,128)(2,1)S(1)}, bf16[64,128]{1,0:T(8,128)(2,1)S(1)}, u32[]{:S(2)}, u32[]{:S(2)}) collective-permute-start(bf16[64,128]{1,0:T(8,128)(2,1)S(1)} %get-tuple-element.41), channel_id=1, source_target_pairs={{0,16},{4,20},{8,24},{12,28},{16,0},{20,4},{24,8},{28,12},{1,17},{... | collective-permute-start | bytes 49160 | tf_op jit(solution)/shard_map/ppermute | solution.py:423
  37.0 3.5 %collective-permute-start.8 = (bf16[64,128]{1,0:T(8,128)(2,1)S(1)}, bf16[64,128]{1,0:T(8,128)(2,1)S(1)}, u32[]{:S(2)}, u32[]{:S(2)}) collective-permute-start(bf16[64,128]{1,0:T(8,128)(2,1)S(1)} %get-tuple-element.42), channel_id=1, source_target_pairs={{0,12},{4,8},{8,4},{12,0},{16,28},{20,24},{24,20},{28,16},{1,13},{... | collective-permute-start | bytes 49160 | tf_op jit(solution)/shard_map/ppermute | solution.py:423
  37.7 3.8 %collective-permute-start.9 = (bf16[64,128]{1,0:T(8,128)(2,1)S(1)}, bf16[64,128]{1,0:T(8,128)(2,1)S(1)}, u32[]{:S(2)}, u32[]{:S(2)}) collective-permute-start(bf16[64,128]{1,0:T(8,128)(2,1)S(1)} %get-tuple-element.43), channel_id=1, source_target_pairs={{0,8},{4,12},{8,0},{12,4},{16,24},{20,28},{24,16},{28,20},{1,9},{5... | collective-permute-start | bytes 49160 | tf_op jit(solution)/shard_map/ppermute | solution.py:423
  38.6 2.9 %collective-permute-start.10 = (bf16[64,128]{1,0:T(8,128)(2,1)S(1)}, bf16[64,128]{1,0:T(8,128)(2,1)S(1)}, u32[]{:S(2)}, u32[]{:S(2)}) collective-permute-start(bf16[64,128]{1,0:T(8,128)(2,1)S(1)} %get-tuple-element.44), channel_id=1, source_target_pairs={{0,4},{4,0},{8,12},{12,8},{16,20},{20,16},{24,28},{28,24},{1,5},{5... | collective-permute-start | bytes 49160 | tf_op jit(solution)/shard_map/ppermute | solution.py:423
  38.8 2.7 %copy-start.3 = (bf16[1024,896]{1,0:T(8,128)(2,1)S(1)}, bf16[1024,896]{1,0:T(8,128)(2,1)}, u32[]{:S(2)}) copy-start(bf16[1024,896]{1,0:T(8,128)(2,1)} %copy-done.2) | copy-start | bytes 5505028
  38.8 2.7 %copy-start.5 = (bf16[1,2,512,512]{3,2,1,0:T(8,128)(2,1)S(1)}, bf16[1,2,512,512]{3,2,1,0:T(8,128)(2,1)}, u32[]{:S(2)}) copy-start(bf16[1,2,512,512]{3,2,1,0:T(8,128)(2,1)} %copy-done.4) | copy-start | bytes 3145732
  38.9 2.7 %copy-start.13 = (bf16[512,256]{1,0:T(8,128)(2,1)S(1)}, bf16[512,256]{1,0:T(8,128)(2,1)}, u32[]{:S(2)}) copy-start(bf16[512,256]{1,0:T(8,128)(2,1)} %copy-done.12) | copy-start | bytes 786436
  44.6 8.6 %copy-start.11 = (bf16[2,256,256]{2,1,0:T(8,128)(2,1)S(1)}, bf16[2,256,256]{2,1,0:T(8,128)(2,1)}, u32[]{:S(2)}) copy-start(bf16[2,256,256]{2,1,0:T(8,128)(2,1)} %copy-done.10) | copy-start | bytes 786436
  44.6 7.7 %collective-permute-start.13 = (bf16[128,256]{1,0:T(8,128)(2,1)S(1)}, bf16[128,256]{1,0:T(8,128)(2,1)S(1)}, u32[]{:S(2)}, u32[]{:S(2)}) collective-permute-start(bf16[128,256]{1,0:T(8,128)(2,1)S(1)} %get-tuple-element.45.refs_0_), channel_id=1, source_target_pairs={{0,2},{1,3},{2,0},{3,1},{4,6},{5,7},{6,4},{7,5},{8,10},{9,11},{10,... | collective-permute-start | bytes 196616 | tf_op jit(solution)/shard_map/ppermute | solution.py:333
  45.7 6.6 %collective-permute-start.12 = (bf16[128,256]{1,0:T(8,128)(2,1)S(1)}, bf16[128,256]{1,0:T(8,128)(2,1)S(1)}, u32[]{:S(2)}, u32[]{:S(2)}) collective-permute-start(bf16[128,256]{1,0:T(8,128)(2,1)S(1)} %get-tuple-element.45.refs_0_), channel_id=1, source_target_pairs={{0,3},{1,2},{2,1},{3,0},{4,7},{5,6},{6,5},{7,4},{8,11},{9,10},{10,... | collective-permute-start | bytes 196616 | tf_op jit(solution)/shard_map/ppermute | solution.py:333
  47.2 6.0 %collective-permute-start.11 = (bf16[128,256]{1,0:T(8,128)(2,1)S(1)}, bf16[128,256]{1,0:T(8,128)(2,1)S(1)}, u32[]{:S(2)}, u32[]{:S(2)}) collective-permute-start(bf16[128,256]{1,0:T(8,128)(2,1)S(1)} %get-tuple-element.45.refs_0_), channel_id=1, source_target_pairs={{0,1},{1,0},{2,3},{3,2},{4,5},{5,4},{6,7},{7,6},{8,9},{9,8},{10,11... | collective-permute-start | bytes 196616 | tf_op jit(solution)/shard_map/ppermute | solution.py:333
